TPU v7x, 32 devices: a whole 2x2x4 slice. The times are simulated.
32 devices in a mesh: mode: 16 (over z, x, core), rank: 2 (over y).
Axes of the slice: x: 2, y: 2, z: 4, core: 2. Of those that a mesh axis runs over, the one named last changes fastest.
Arguments:
- start_core: float32 [256, 128, 128], P('mode', 'rank'), may hold values from -108 to 108
- right_side: float32 [256, 128, 128], P('mode', 'rank'), may hold values from -108 to 108
- left_interface: float32 [3, 128, 128], replicated, may hold values from -1 to 2
- right_interface: float32 [3, 128, 128], replicated, may hold values from -1 to 2
- couplings: float32 [3, 3, 3, 256], P(None, None, None, 'mode'), may hold values from -5 to 5
Outputs:
- orthonormal_core: float32 [256, 128, 128], P('mode', 'rank')
- triangle: float32 [128, 128], replicated
- next_interface: float32 [3, 128, 128], P(None, 'rank')
All inputs are finite; a program needn't handle non-finite values.
Results may differ from a plain program's by a relative error of at most 0.00027.
Values sent between devices are 32-bit elements; how exact they have to be, the bound alone decides.
A program may use at most 64 MiB of HBM per device.

v0:
```python
import functools

import jax
import jax.numpy as jnp
from jax import lax
from jax.experimental import pallas as pl
from jax.experimental.pallas import tpu as pltpu
from jax.sharding import PartitionSpec as P

HIGH = lax.Precision.HIGH
HIGHEST = lax.Precision.HIGHEST
F32 = jnp.float32


def dot(a, b, dims=((1,), (0,)), precision=HIGH):
    return lax.dot_general(a, b, (dims, ((), ())), precision=precision, preferred_element_type=F32)


def contract_right(source, weights, target, count, width):
    def body(p, carry):
        pair = jnp.concatenate([source[2 * p], source[2 * p + 1]], axis=1)
        out = dot(weights[...], pair)
        for k in range(3):
            rows = out[k * width : (k + 1) * width]
            target[k, 2 * p] = rows[:, :width]
            target[k, 2 * p + 1] = rows[:, width:]
        return carry

    lax.fori_loop(0, count // 2, body, 0)


def coupled(field, factors, row, index, inner_first, width):
    step = min(64, width)
    pieces = []
    for start in range(0, width, step):
        sums = [None] * 3
        for k in range(3):
            for s in range(3):
                block = field[k, index + s, start : start + step, :]
                for o in range(3):
                    pair = (k * 3 + o) if inner_first else (o * 3 + k)
                    term = factors[row, pl.ds(pair * 3 + s, 1), :] * block
                    sums[o] = term if sums[o] is None else sums[o] + term
        pieces.append(sums)
    return [jnp.concatenate([piece[o] for piece in pieces], axis=0) for o in range(3)]


def eliminate(work, width):
    size = 8
    sub = lax.broadcasted_iota(jnp.int32, (size, 2 * width), 0)
    for k in range(width // size):
        base = k * size
        panel = work[base : base + size, :]
        rows = [jnp.broadcast_to(panel[i : i + 1, :], (size, 2 * width)) for i in range(size)]
        entry = {}
        for j in range(size):
            column = jnp.broadcast_to(panel[:, base + j : base + j + 1], (size, width))
            for i in range(j, size):
                entry[i, j] = jnp.broadcast_to(column[i : i + 1, :], (size, width))
        for j in range(size):
            pivot = entry[j, j]
            inv = lax.rsqrt(pivot)
            inv = inv * (1.5 - 0.5 * (pivot * inv) * inv)
            rows[j] = rows[j] * jnp.concatenate([inv, inv], axis=1)
            scaled = {i: entry[i, j] * inv for i in range(j + 1, size)}
            for c in range(j + 1, size):
                for i in range(c, size):
                    entry[i, c] = entry[i, c] - scaled[i] * scaled[c]
            for i in range(j + 1, size):
                factor = jnp.concatenate([scaled[i], scaled[i]], axis=1)
                rows[i] = rows[i] - factor * rows[j]
        done = rows[0]
        for i in range(1, size):
            done = jnp.where(sub == i, rows[i], done)
        work[base : base + size, :] = done
        if base + size < width:
            update = dot(done[:, :width], done, ((0,), (0,)), HIGHEST)
            work[base + size :, :] = work[base + size :, :] - update[base + size :, :]


def kernel(
    nm, nr, ml, scale,
    x_ref, f_ref, l_ref, p_ref, c_ref,
    q_out, tri_out, n_out,
    xf, ff, ce, tt, res, qb, lt_rows, lt_cols, work,
    gpart, grecv, gsend, gbrecv, gfull,
    ssend, srecv, sbsend, sbrecv,
    npart, nrecv, nsend, nbrecv, nfull,
    x_send, x_recv, xe_send, xe_recv,
    f_send, f_recv, fe_send, fe_recv,
    ce_send, ce_recv,
    ga_send, ga_recv, gb_send, gb_recv, gc_send, gc_recv,
    sa_send, sa_recv, sb_send, sb_recv,
    na_send, na_recv, nb_send, nb_recv, nc_send, nc_recv,
    q_send, q_recv,
):
    height, piece, width = x_ref.shape
    mine = height // nr
    mh = nm // ml
    na = nr * ml
    m = lax.axis_index("mode")
    r = lax.axis_index("rank")
    low = lax.rem(m, ml)
    high = lax.div(m, ml)
    g = r * ml + low
    has_prev = m > 0
    has_next = m < nm - 1

    def at_a(t):
        return {"mode": high * ml + lax.rem(t, ml), "rank": lax.div(t, ml)}

    def at_b(t):
        return {"mode": t * ml + low, "rank": r}

    def at_r(t):
        return {"mode": m, "rank": t}

    def remote(src, dst, send, recv, where):
        return pltpu.make_async_remote_copy(
            src_ref=src, dst_ref=dst, send_sem=send, recv_sem=recv,
            device_id=where, device_id_type=pl.DeviceIdType.MESH,
        )

    def greet(where):
        pl.semaphore_signal(
            barrier, inc=1, device_id=where, device_id_type=pl.DeviceIdType.MESH
        )

    barrier = pltpu.get_barrier_semaphore()
    for d in range(1, na):
        greet(at_a(lax.rem(g + d, na)))
    for d in range(1, mh):
        greet(at_b(lax.rem(high + d, mh)))

    @pl.when(has_prev)
    def _():
        for t in range(nr):
            greet({"mode": m - 1, "rank": t})

    @pl.when(has_next)
    def _():
        for t in range(nr):
            greet({"mode": m + 1, "rank": t})

    pl.semaphore_wait(
        barrier, na - 1 + mh - 1 + nr * (has_prev.astype(jnp.int32) + has_next.astype(jnp.int32))
    )

    columns = pl.ds(pl.multiple_of(r * piece, piece), piece)

    def span(t, halo):
        first = max(0, mine * t - halo)
        last = min(height, mine * t + mine + halo)
        return first, last - first, first - (mine * t - halo)

    moves = []
    for source, target, halo, send, recv, esend, erecv in (
        (x_ref, xf, 2, x_send, x_recv, xe_send, xe_recv),
        (f_ref, ff, 1, f_send, f_recv, fe_send, fe_recv),
    ):
        up = remote(
            source.at[pl.ds(height - halo, halo)], target.at[pl.ds(0, halo), columns],
            esend.at[0], erecv.at[r], {"mode": m + 1, "rank": 0},
        )
        down = remote(
            source.at[pl.ds(0, halo)], target.at[pl.ds(mine + halo, halo), columns],
            esend.at[1], erecv.at[r], {"mode": m - 1, "rank": nr - 1},
        )
        pl.when(has_next)(up.start)
        pl.when(has_prev)(down.start)
        across = []
        for t in range(nr):
            first, count, offset = span(t, halo)
            copy = remote(
                source.at[pl.ds(first, count)], target.at[pl.ds(offset, count), columns],
                send.at[t], recv.at[r], at_r(t),
            )
            pl.when(r != t)(copy.start)
            across.append(copy)
        moves.append((up, down, across))
        if source is x_ref:
            c_up = remote(
                c_ref.at[pl.ds(height - 1, 1)], ce.at[pl.ds(0, 1)],
                ce_send.at[0], ce_recv.at[0], {"mode": m + 1, "rank": r},
            )
            c_down = remote(
                c_ref.at[pl.ds(0, 1)], ce.at[pl.ds(mine + 1, 1)],
                ce_send.at[1], ce_recv.at[1], {"mode": m - 1, "rank": r},
            )
            pl.when((r == 0) & has_next)(c_up.start)
            pl.when((r == nr - 1) & has_prev)(c_down.start)

    for t in range(nr):

        @pl.when(r == t)
        def _():
            for source, target, halo in ((x_ref, xf, 2), (f_ref, ff, 1)):
                first, count, offset = span(t, halo)
                target[offset : offset + count, t * piece : (t + 1) * piece, :] = source[
                    first : first + count
                ]
            first, count, offset = span(t, 1)
            ce[offset : offset + count] = c_ref[first : first + count]

    @pl.when((r == 0) & jnp.logical_not(has_prev))
    def _():
        xf[0:2] = jnp.zeros((2, width, width), F32)
        ff[0:1] = jnp.zeros((1, width, width), F32)
        ce[0:1] = jnp.zeros((1,) + ce.shape[1:], F32)

    @pl.when((r == nr - 1) & jnp.logical_not(has_next))
    def _():
        xf[mine + 2 :] = jnp.zeros((2, width, width), F32)
        ff[mine + 1 :] = jnp.zeros((1, width, width), F32)
        ce[mine + 1 :] = jnp.zeros((1,) + ce.shape[1:], F32)

    for k in range(3):
        turned = l_ref[k].T
        lt_rows[k * width : (k + 1) * width, :] = turned
        lt_cols[:, k * width : (k + 1) * width] = turned

    low_edge = (r == 0) & has_prev
    high_edge = (r == nr - 1) & has_next

    def arrive(target, halo, recv, erecv, send, esend):
        for t in range(nr):
            part = pl.ds(t * piece, piece)
            for mine_rank in range(nr):
                if mine_rank == t:
                    continue
                _, count, offset = span(mine_rank, halo)
                block = target.at[pl.ds(offset, count), part]
                pl.when(r == mine_rank)(
                    remote(block, block, send.at[t], recv.at[t], at_r(t)).wait_recv
                )
            block = target.at[pl.ds(0, halo), part]
            pl.when(low_edge)(remote(block, block, esend.at[0], erecv.at[t], at_r(t)).wait_recv)
            block = target.at[pl.ds(mine + halo, halo), part]
            pl.when(high_edge)(remote(block, block, esend.at[1], erecv.at[t], at_r(t)).wait_recv)

    arrive(xf, 2, x_recv, xe_recv, x_send, xe_send)
    pl.when(low_edge)(c_up.wait_recv)
    pl.when(high_edge)(c_down.wait_recv)

    contract_right(xf, p_ref, tt, mine + 4, width)
    arrive(ff, 1, f_recv, fe_recv, f_send, fe_send)

    def applied(index, row):
        parts = coupled(tt, ce, row, index, False, width)
        return dot(jnp.concatenate(parts, axis=1), lt_rows[...])

    def residual_body(i, carry):
        res[i] = ff[i] - applied(i, i)
        return carry

    lax.fori_loop(0, mine + 2, residual_body, 0)

    def gram_body(i, total):
        both = jnp.concatenate([xf[i + 2], res[i + 1]], axis=0)
        return total + dot(both, both, ((1,), (1,)))

    total = lax.fori_loop(0, mine, gram_body, jnp.zeros((2 * width, 2 * width), F32))
    cross = total[:width, width:]
    pieces = jnp.concatenate(
        [total[:width, :width], cross + cross.T, total[width:, width:]], axis=0
    )
    gpart[...] = pieces.reshape(gpart.shape)

    def scatter(part, recv_buf, send, recv):
        for d in range(1, na):
            t = lax.rem(g + d, na)
            remote(part.at[t], recv_buf.at[g], send.at[d - 1], recv.at[d - 1], at_a(t)).start()
        recv_buf[g] = part[g]

    def spread(part, recv_buf, send, recv):
        for d in range(1, na):
            t = lax.rem(g + d, na)
            remote(part, recv_buf.at[g], send.at[d - 1], recv.at[d - 1], at_a(t)).start()
        recv_buf[g] = part[...]

    def gathered(recv_buf, send, recv):
        for d in range(1, na):
            t = lax.rem(g + na - d, na)
            block = recv_buf.at[t]
            remote(block, block, send.at[d - 1], recv.at[d - 1], at_a(t)).wait_recv()

    def exchange_b(part, recv_buf, send, recv):
        for d in range(1, mh):
            t = lax.rem(high + d, mh)
            remote(part, recv_buf.at[high], send.at[d - 1], recv.at[d - 1], at_b(t)).start()
        recv_buf[high] = part[...]

    def gathered_b(recv_buf, send, recv):
        for d in range(1, mh):
            t = lax.rem(high + mh - d, mh)
            block = recv_buf.at[t]
            remote(block, block, send.at[d - 1], recv.at[d - 1], at_b(t)).wait_recv()

    def add_up(recv_buf, count):
        out = recv_buf[0]
        for t in range(1, count):
            out = out + recv_buf[t]
        return out

    scatter(gpart, grecv, ga_send, ga_recv)
    contract_right(res, p_ref, tt, mine + 2, width)
    gathered(grecv, ga_send, ga_recv)
    gsend[...] = add_up(grecv, na)
    exchange_b(gsend, gbrecv, gb_send, gb_recv)

    def fold(values):
        return jnp.sum(values.reshape(width // 8, 8, width), axis=0)

    def image_body(i, carry):
        along, energy = carry
        image = applied(i, i + 1)
        return along + fold(res[i + 1] * image), energy + fold(image * image)

    zero = jnp.zeros((8, width), F32)
    along, energy = lax.fori_loop(0, mine, image_body, (zero, zero))
    ssend[0:1, :] = jnp.sum(along, axis=0, keepdims=True)
    ssend[1:2, :] = jnp.sum(energy, axis=0, keepdims=True)
    ssend[2:8, :] = jnp.zeros((6, width), F32)
    spread(ssend, srecv, sa_send, sa_recv)
    gathered_b(gbrecv, gb_send, gb_recv)
    gfull[g] = add_up(gbrecv, mh)
    for d in range(1, na):
        t = lax.rem(g + d, na)
        remote(gfull.at[g], gfull.at[g], gc_send.at[d - 1], gc_recv.at[d - 1], at_a(t)).start()
    gathered(srecv, sa_send, sa_recv)
    sbsend[...] = add_up(srecv, na)
    exchange_b(sbsend, sbrecv, sb_send, sb_recv)
    gathered(gfull, gc_send, gc_recv)
    gathered_b(sbrecv, sb_send, sb_recv)
    sums = jnp.sum(add_up(sbrecv, mh), axis=1, keepdims=True)
    alpha = sums[0:1, :] / sums[1:2, :]

    grams = gfull[...].reshape(3 * width, width)
    gram = (
        grams[:width] + alpha * grams[width : 2 * width] + (alpha * alpha) * grams[2 * width :]
    ) * scale
    rows = lax.broadcasted_iota(jnp.int32, (width, width), 0)
    lanes = lax.broadcasted_iota(jnp.int32, (width, width), 1)
    work[:, :width] = gram
    work[:, width:] = jnp.where(rows == lanes, 1.0, 0.0).astype(F32)
    eliminate(work, width)
    tri_out[...] = jnp.where(lanes >= rows, work[:, :width], 0.0)
    inverse = jnp.where(lanes <= rows, work[:, width:], 0.0)

    def basis_body(p, carry):
        pair = jnp.concatenate(
            [xf[2 * p + 1] + alpha * res[2 * p], xf[2 * p + 2] + alpha * res[2 * p + 1]], axis=1
        )
        out = dot(inverse, pair)
        qb[2 * p] = out[:, :width]
        qb[2 * p + 1] = out[:, width:]
        return carry

    lax.fori_loop(0, (mine + 2) // 2, basis_body, 0)
    slab = pl.ds(r * mine, mine)
    for d in range(1, nr):
        t = lax.rem(r + d, nr)
        remote(
            qb.at[pl.ds(1, mine), pl.ds(pl.multiple_of(t * piece, piece), piece)],
            q_out.at[slab], q_send.at[d - 1], q_recv.at[d - 1], at_r(t),
        ).start()

    def mixed_body(i, carry):
        out = dot(qb[i], lt_cols[...])
        for k in range(3):
            tt[k, i] = out[:, k * width : (k + 1) * width]
        return carry

    lax.fori_loop(0, mine + 2, mixed_body, 0)

    def interface_body(i, total):
        parts = coupled(tt, ce, i + 1, i, True, width)
        return total + dot(jnp.concatenate(parts, axis=0), qb[i + 1], ((1,), (1,)))

    total = lax.fori_loop(0, mine, interface_body, jnp.zeros((3 * width, width), F32)) * scale
    total = total.reshape(3, nr, piece, width)
    for t in range(nr):
        npart[t * ml : (t + 1) * ml] = total[:, t].reshape((ml,) + npart.shape[1:])
    scatter(npart, nrecv, na_send, na_recv)
    q_out[slab] = qb[1 : mine + 1, columns, :]
    gathered(nrecv, na_send, na_recv)
    nsend[...] = add_up(nrecv, na)
    exchange_b(nsend, nbrecv, nb_send, nb_recv)
    gathered_b(nbrecv, nb_send, nb_recv)
    nfull[low] = add_up(nbrecv, mh)

    def at_c(t):
        return {"mode": high * ml + t, "rank": r}

    for d in range(1, ml):
        t = lax.rem(low + d, ml)
        remote(
            nfull.at[low], nfull.at[low], nc_send.at[d - 1], nc_recv.at[d - 1], at_c(t)
        ).start()
    for d in range(1, ml):
        t = lax.rem(low + ml - d, ml)
        block = nfull.at[t]
        remote(block, block, nc_send.at[d - 1], nc_recv.at[d - 1], at_c(t)).wait_recv()
    n_out[...] = nfull[...]

    for d in range(1, nr):
        t = lax.rem(r + nr - d, nr)
        block = q_out.at[pl.ds(t * mine, mine)]
        remote(block, block, q_send.at[d - 1], q_recv.at[d - 1], at_r(t)).wait_recv()

    for up, down, across in moves:
        pl.when(has_next)(up.wait_send)
        pl.when(has_prev)(down.wait_send)
        for t in range(nr):
            pl.when(r != t)(across[t].wait_send)
    pl.when((r == 0) & has_next)(c_up.wait_send)
    pl.when((r == nr - 1) & has_prev)(c_down.wait_send)
    for send, block, count in (
        (ga_send, gpart.at[0], na), (gc_send, gfull.at[0], na), (sa_send, ssend, na),
        (na_send, npart.at[0], na), (gb_send, gsend, mh), (sb_send, sbsend, mh),
        (nb_send, nsend, mh), (nc_send, nfull.at[0], ml), (q_send, q_out.at[pl.ds(0, mine)], nr),
    ):
        for d in range(1, count):
            remote(block, block, send.at[d - 1], send.at[d - 1], at_r(r)).wait_send()


def shards(nm, nr, start_core, right_side, left_interface, right_interface, couplings):
    height, piece, width = start_core.shape
    mine = height // nr
    ml = max(1, min(nm, 8 // nr))
    mh = nm // ml
    na = nr * ml
    scale = 1.0 / (height * nm * width)
    flat = couplings.reshape(27, height).T
    spread = jnp.broadcast_to(
        jnp.pad(flat, ((0, 0), (0, 5)))[:, :, None], (height, 32, width)
    )
    grows = 3 * width // na
    nrows = 3 * piece // ml
    vmem = lambda *shape: pltpu.VMEM(shape, F32)
    sem = lambda count: pltpu.SemaphoreType.DMA((max(1, count),))
    scratch = [
        vmem(mine + 4, width, width), vmem(mine + 2, width, width), vmem(mine + 2, 32, width),
        vmem(3, mine + 4, width, width), vmem(mine + 2, width, width),
        vmem(mine + 2, width, width), vmem(3 * width, width), vmem(width, 3 * width),
        vmem(width, 2 * width),
        vmem(na, grows, width), vmem(na, grows, width), vmem(grows, width),
        vmem(mh, grows, width), vmem(na, grows, width),
        vmem(8, width), vmem(na, 8, width), vmem(8, width), vmem(mh, 8, width),
        vmem(na, nrows, width), vmem(na, nrows, width), vmem(nrows, width),
        vmem(mh, nrows, width), vmem(ml, nrows, width),
        sem(nr), sem(nr), sem(2), sem(nr),
        sem(nr), sem(nr), sem(2), sem(nr),
        sem(2), sem(2),
        sem(na), sem(na), sem(mh), sem(mh), sem(na), sem(na),
        sem(na), sem(na), sem(mh), sem(mh),
        sem(na), sem(na), sem(mh), sem(mh), sem(ml), sem(ml),
        sem(nr), sem(nr),
    ]
    space = pl.BlockSpec(memory_space=pltpu.VMEM)
    basis, triangle, interface = pl.pallas_call(
        functools.partial(kernel, nm, nr, ml, scale),
        out_shape=(
            jax.ShapeDtypeStruct((height, piece, width), F32),
            jax.ShapeDtypeStruct((width, width), F32),
            jax.ShapeDtypeStruct((ml, nrows, width), F32),
        ),
        in_specs=[space] * 5,
        out_specs=(space,) * 3,
        scratch_shapes=scratch,
        compiler_params=pltpu.CompilerParams(
            collective_id=0, has_side_effects=True, vmem_limit_bytes=40 * 1024 * 1024
        ),
    )(
        start_core, right_side, left_interface,
        right_interface.reshape(3 * width, width), spread,
    )
    return basis, triangle, interface.reshape(3, piece, width)


def solution(mesh):
    placed = (
        P("mode", "rank", None),
        P("mode", "rank", None),
        P(),
        P(),
        P(None, None, None, "mode"),
    )
    return jax.shard_map(
        functools.partial(shards, mesh.shape["mode"], mesh.shape["rank"]),
        mesh=mesh,
        in_specs=placed,
        out_specs=(P("mode", "rank", None), P(), P(None, "rank", None)),
        check_vma=False,
    )
```

profile of v0, /device:TPU:0, one launch (start us, length us, event | category | flops | bytes accessed | tf_op | source)
XLA Modules:
  0.0 74.5 jit_solution(12557579231265130411)
XLA Ops:
  0.6 0.0 copy-start.2
  0.6 0.8 %reshape.17 = f32[27,16]{1,0:T(8,128)S(1)} reshape(f32[3,3,3,16]{3,2,1,0:T(4,128)} %param.9) | data formatting | bytes 3456 | tf_op jit(solution)/shard_map/reshape | solution.py:434
  1.4 0.1 copy.10
  1.5 0.1 broadcast_in_dim.2.c_ref
  1.6 0.0 copy-done.2
  1.6 0.0 copy-start
  1.7 1.0 %copy-done = f32[16,64,128]{2,1,0:T(8,128)S(1)} copy-done((f32[16,64,128]{2,1,0:T(8,128)S(1)}, f32[16,64,128]{2,1,0:T(8,128)}, u32[]{:S(2)}) %copy-start) | copy-done | bytes 524312
  2.7 0.0 copy-start.1
  2.7 1.0 %copy-done.1 = f32[16,64,128]{2,1,0:T(8,128)S(1)} copy-done((f32[16,64,128]{2,1,0:T(8,128)S(1)}, f32[16,64,128]{2,1,0:T(8,128)}, u32[]{:S(2)}) %copy-start.1) | copy-done | bytes 524312
  3.7 0.0 copy-start.3
  3.7 0.9 %copy-done.3 = f32[3,128,128]{2,1,0:T(8,128)S(1)} copy-done((f32[3,128,128]{2,1,0:T(8,128)S(1)}, f32[3,128,128]{2,1,0:T(8,128)}, u32[]{:S(2)}) %copy-start.3) | copy-done | bytes 196632
  4.7 67.8 %shard_map.76 = (f32[16,64,128]{2,1,0:T(8,128)S(1)}, f32[128,128]{1,0:T(8,128)S(1)}, f32[4,48,128]{2,1,0:T(8,128)S(1)}) custom-call(f32[16,64,128]{2,1,0:T(8,128)S(1)} %copy-done, f32[16,64,128]{2,1,0:T(8,128)S(1)} %copy-done.1, f32[3,128,128]{2,1,0:T(8,128)S(1)} %copy-done.2, f32[384,128]{1,0:T(8,128)S(1)} %bitcast.3, f32[16,32,128]{2,1,0:T(8,128)S(1)} %broadcast_in_dim.2.c_ref), custom_call_target="tpu_custom_call" | custom-call | tf_op jit(solution)/shard_map/pallas_call | solution.py:461
  72.4 0.8 %copy.14 = f32[16,64,128]{2,1,0:T(8,128)} copy(f32[16,64,128]{2,1,0:T(8,128)S(1)} %get-tuple-element.12) | data formatting | bytes 1048576
  73.2 0.6 copy.15
  73.8 0.6 copy.16
  (1 shorter events, 0.0 us)
Async XLA Ops:
  0.6 1.0 %copy-start.2 = (f32[3,128,128]{2,1,0:T(8,128)S(1)}, f32[3,128,128]{2,1,0:T(8,128)}, u32[]{:S(2)}) copy-start(f32[3,128,128]{2,1,0:T(8,128)} %l_ref.1) | copy-start | bytes 589828
  1.6 1.0 %copy-start = (f32[16,64,128]{2,1,0:T(8,128)S(1)}, f32[16,64,128]{2,1,0:T(8,128)}, u32[]{:S(2)}) copy-start(f32[16,64,128]{2,1,0:T(8,128)} %x_ref.1) | copy-start | bytes 1572868
  2.7 1.0 %copy-start.1 = (f32[16,64,128]{2,1,0:T(8,128)S(1)}, f32[16,64,128]{2,1,0:T(8,128)}, u32[]{:S(2)}) copy-start(f32[16,64,128]{2,1,0:T(8,128)} %f_ref.1) | copy-start | bytes 1572868
  3.7 0.9 %copy-start.3 = (f32[3,128,128]{2,1,0:T(8,128)S(1)}, f32[3,128,128]{2,1,0:T(8,128)}, u32[]{:S(2)}) copy-start(f32[3,128,128]{2,1,0:T(8,128)} %param.8) | copy-start | bytes 589828
where the time goes:
time: 74.7 us; the launch traced here: 74.5 us
  Pallas kernels  67.8 us (91%)
  local copies, waits for them, and re-layouts  6.06 us (8%)
    pallas_call x1, Pallas kernels, shards(): pl.pallas_call(functools.partial(kernel, nm, nr, ml, scale), out_shape=(j...  67.8 us
    unnamed x12, local copies, waits for them, and re-layouts  5.15 us

commit v1 on v0

--- a/solution.py
+++ b/solution.py
@@ -43,6 +43,10 @@
                     sums[o] = term if sums[o] is None else sums[o] + term
         pieces.append(sums)
     return [jnp.concatenate([piece[o] for piece in pieces], axis=0) for o in range(3)]
+
+
+def coupled_pair(field, factors, row, index, inner_first, width):
+    return [coupled(field, factors, row + d, index + d, inner_first, width) for d in range(2)]
 
 
 def eliminate(work, width):
@@ -80,8 +84,9 @@
 
 def kernel(
     nm, nr, ml, scale,
-    x_ref, f_ref, l_ref, p_ref, c_ref,
+    x_ref, f_ref, l_hbm, p_hbm, raw_ref,
     q_out, tri_out, n_out,
+    l_ref, p_ref, c_ref, own_sem,
     xf, ff, ce, tt, res, qb, lt_rows, lt_cols, work,
     gpart, grecv, gsend, gbrecv, gfull,
     ssend, srecv, sbsend, sbrecv,
@@ -126,6 +131,11 @@
             barrier, inc=1, device_id=where, device_id_type=pl.DeviceIdType.MESH
         )
 
+    fetch_l = pltpu.make_async_copy(l_hbm, l_ref, own_sem.at[0])
+    fetch_p = pltpu.make_async_copy(p_hbm, p_ref, own_sem.at[1])
+    fetch_l.start()
+    fetch_p.start()
+
     barrier = pltpu.get_barrier_semaphore()
     for d in range(1, na):
         greet(at_a(lax.rem(g + d, na)))
@@ -141,6 +151,13 @@
     def _():
         for t in range(nr):
             greet({"mode": m + 1, "rank": t})
+
+    for o in range(3):
+        for k in range(3):
+            block = raw_ref[o, k]
+            first = (o * 3 + k) * 3
+            for i in range(height):
+                c_ref[i, first : first + 3, :] = jnp.broadcast_to(block[:, i : i + 1], (3, width))
 
     pl.semaphore_wait(
         barrier, na - 1 + mh - 1 + nr * (has_prev.astype(jnp.int32) + has_next.astype(jnp.int32))
@@ -194,11 +211,15 @@
 
         @pl.when(r == t)
         def _():
-            for source, target, halo in ((x_ref, xf, 2), (f_ref, ff, 1)):
+            for source, target, halo, sem in (
+                (x_ref, xf, 2, own_sem.at[2]), (f_ref, ff, 1, own_sem.at[3])
+            ):
                 first, count, offset = span(t, halo)
-                target[offset : offset + count, t * piece : (t + 1) * piece, :] = source[
-                    first : first + count
-                ]
+                pltpu.make_async_copy(
+                    source.at[pl.ds(first, count)],
+                    target.at[pl.ds(offset, count), pl.ds(t * piece, piece)],
+                    sem,
+                ).start()
             first, count, offset = span(t, 1)
             ce[offset : offset + count] = c_ref[first : first + count]
 
@@ -214,6 +235,7 @@
         ff[mine + 1 :] = jnp.zeros((1, width, width), F32)
         ce[mine + 1 :] = jnp.zeros((1,) + ce.shape[1:], F32)
 
+    fetch_l.wait()
     for k in range(3):
         turned = l_ref[k].T
         lt_rows[k * width : (k + 1) * width, :] = turned
@@ -222,9 +244,12 @@
     low_edge = (r == 0) & has_prev
     high_edge = (r == nr - 1) & has_next
 
-    def arrive(target, halo, recv, erecv, send, esend):
+    def arrive(target, halo, recv, erecv, send, esend, own):
         for t in range(nr):
             part = pl.ds(t * piece, piece)
+            _, count, offset = span(t, halo)
+            block = target.at[pl.ds(offset, count), part]
+            pl.when(r == t)(pltpu.make_async_copy(block, block, own).wait)
             for mine_rank in range(nr):
                 if mine_rank == t:
                     continue
@@ -238,28 +263,39 @@
             block = target.at[pl.ds(mine + halo, halo), part]
             pl.when(high_edge)(remote(block, block, esend.at[1], erecv.at[t], at_r(t)).wait_recv)
 
-    arrive(xf, 2, x_recv, xe_recv, x_send, xe_send)
+    arrive(xf, 2, x_recv, xe_recv, x_send, xe_send, own_sem.at[2])
     pl.when(low_edge)(c_up.wait_recv)
     pl.when(high_edge)(c_down.wait_recv)
 
+    fetch_p.wait()
     contract_right(xf, p_ref, tt, mine + 4, width)
-    arrive(ff, 1, f_recv, fe_recv, f_send, fe_send)
+    arrive(ff, 1, f_recv, fe_recv, f_send, fe_send, own_sem.at[3])
 
     def applied(index, row):
-        parts = coupled(tt, ce, row, index, False, width)
-        return dot(jnp.concatenate(parts, axis=1), lt_rows[...])
-
-    def residual_body(i, carry):
-        res[i] = ff[i] - applied(i, i)
+        pair = coupled_pair(tt, ce, row, index, False, width)
+        stacked = jnp.concatenate([jnp.concatenate(parts, axis=1) for parts in pair], axis=0)
+        return dot(stacked, lt_rows[...])
+
+    def residual_body(p, carry):
+        out = applied(2 * p, 2 * p)
+        res[2 * p] = ff[2 * p] - out[:width]
+        res[2 * p + 1] = ff[2 * p + 1] - out[width:]
         return carry
 
-    lax.fori_loop(0, mine + 2, residual_body, 0)
-
-    def gram_body(i, total):
-        both = jnp.concatenate([xf[i + 2], res[i + 1]], axis=0)
+    lax.fori_loop(0, (mine + 2) // 2, residual_body, 0)
+
+    def gram_body(p, total):
+        i = 2 * p
+        both = jnp.concatenate(
+            [
+                jnp.concatenate([xf[i + 2], xf[i + 3]], axis=1),
+                jnp.concatenate([res[i + 1], res[i + 2]], axis=1),
+            ],
+            axis=0,
+        )
         return total + dot(both, both, ((1,), (1,)))
 
-    total = lax.fori_loop(0, mine, gram_body, jnp.zeros((2 * width, 2 * width), F32))
+    total = lax.fori_loop(0, mine // 2, gram_body, jnp.zeros((2 * width, 2 * width), F32))
     cross = total[:width, width:]
     pieces = jnp.concatenate(
         [total[:width, :width], cross + cross.T, total[width:, width:]], axis=0
@@ -311,13 +347,15 @@
     def fold(values):
         return jnp.sum(values.reshape(width // 8, 8, width), axis=0)
 
-    def image_body(i, carry):
+    def image_body(p, carry):
         along, energy = carry
-        image = applied(i, i + 1)
-        return along + fold(res[i + 1] * image), energy + fold(image * image)
+        image = applied(2 * p, 2 * p + 1)
+        along = along + fold(res[2 * p + 1] * image[:width])
+        along = along + fold(res[2 * p + 2] * image[width:])
+        return along, energy + fold(image[:width] * image[:width] + image[width:] * image[width:])
 
     zero = jnp.zeros((8, width), F32)
-    along, energy = lax.fori_loop(0, mine, image_body, (zero, zero))
+    along, energy = lax.fori_loop(0, mine // 2, image_body, (zero, zero))
     ssend[0:1, :] = jnp.sum(along, axis=0, keepdims=True)
     ssend[1:2, :] = jnp.sum(energy, axis=0, keepdims=True)
     ssend[2:8, :] = jnp.zeros((6, width), F32)
@@ -365,19 +403,23 @@
             q_out.at[slab], q_send.at[d - 1], q_recv.at[d - 1], at_r(t),
         ).start()
 
-    def mixed_body(i, carry):
-        out = dot(qb[i], lt_cols[...])
+    def mixed_body(p, carry):
+        out = dot(jnp.concatenate([qb[2 * p], qb[2 * p + 1]], axis=0), lt_cols[...])
         for k in range(3):
-            tt[k, i] = out[:, k * width : (k + 1) * width]
+            tt[k, 2 * p] = out[:width, k * width : (k + 1) * width]
+            tt[k, 2 * p + 1] = out[width:, k * width : (k + 1) * width]
         return carry
 
-    lax.fori_loop(0, mine + 2, mixed_body, 0)
-
-    def interface_body(i, total):
-        parts = coupled(tt, ce, i + 1, i, True, width)
-        return total + dot(jnp.concatenate(parts, axis=0), qb[i + 1], ((1,), (1,)))
-
-    total = lax.fori_loop(0, mine, interface_body, jnp.zeros((3 * width, width), F32)) * scale
+    lax.fori_loop(0, (mine + 2) // 2, mixed_body, 0)
+
+    def interface_body(p, total):
+        i = 2 * p
+        pair = coupled_pair(tt, ce, i + 1, i, True, width)
+        moved = jnp.concatenate([jnp.concatenate(parts, axis=0) for parts in pair], axis=1)
+        basis = jnp.concatenate([qb[i + 1], qb[i + 2]], axis=1)
+        return total + dot(moved, basis, ((1,), (1,)))
+
+    total = lax.fori_loop(0, mine // 2, interface_body, jnp.zeros((3 * width, width), F32)) * scale
     total = total.reshape(3, nr, piece, width)
     for t in range(nr):
         npart[t * ml : (t + 1) * ml] = total[:, t].reshape((ml,) + npart.shape[1:])
@@ -431,16 +473,13 @@
     mh = nm // ml
     na = nr * ml
     scale = 1.0 / (height * nm * width)
-    flat = couplings.reshape(27, height).T
-    spread = jnp.broadcast_to(
-        jnp.pad(flat, ((0, 0), (0, 5)))[:, :, None], (height, 32, width)
-    )
     grows = 3 * width // na
     nrows = 3 * piece // ml
     vmem = lambda *shape: pltpu.VMEM(shape, F32)
     sem = lambda count: pltpu.SemaphoreType.DMA((max(1, count),))
     scratch = [
-        vmem(mine + 4, width, width), vmem(mine + 2, width, width), vmem(mine + 2, 32, width),
+        vmem(3, width, width), vmem(3 * width, width), vmem(height, 27, width), sem(4),
+        vmem(mine + 4, width, width), vmem(mine + 2, width, width), vmem(mine + 2, 27, width),
         vmem(3, mine + 4, width, width), vmem(mine + 2, width, width),
         vmem(mine + 2, width, width), vmem(3 * width, width), vmem(width, 3 * width),
         vmem(width, 2 * width),
@@ -465,7 +504,7 @@
             jax.ShapeDtypeStruct((width, width), F32),
             jax.ShapeDtypeStruct((ml, nrows, width), F32),
         ),
-        in_specs=[space] * 5,
+        in_specs=[pl.BlockSpec(memory_space=pl.ANY)] * 4 + [space],
         out_specs=(space,) * 3,
         scratch_shapes=scratch,
         compiler_params=pltpu.CompilerParams(
@@ -473,7 +512,7 @@
         ),
     )(
         start_core, right_side, left_interface,
-        right_interface.reshape(3 * width, width), spread,
+        right_interface.reshape(3 * width, width), couplings,
     )
     return basis, triangle, interface.reshape(3, piece, width)
 

time: 74.7 us -> 74.6 us (level)
  Pallas kernels: 67.8 us -> 66.9 us
    unnamed x12 -> x13, local copies, waits for them, and re-layouts: 5.15 us -> 6.71 us
    pallas_call x1, Pallas kernels: 67.8 us -> 66.9 us  [shards(): pl.pallas_call(functools.partial(kernel, nm, nr, ml, scale), out_shape=(j...]
    reshape x1 -> x0, local copies, waits for them, and re-layouts: 0.77 us -> none  [shards(): flat = couplings.reshape(27, height).T]
where the time goes in v1:
time: 74.6 us; the launch traced here: 74.3 us
  Pallas kernels  66.9 us (90%)
  local copies, waits for them, and re-layouts  6.71 us (9%)
    pallas_call x1, Pallas kernels, shards(): pl.pallas_call(functools.partial(kernel, nm, nr, ml, scale), out_shape=(j...  66.9 us
    unnamed x13, local copies, waits for them, and re-layouts  6.71 us

profile of v1, /device:TPU:0, one launch (start us, length us, event | category | flops | bytes accessed | tf_op | source)
XLA Modules:
  0.0 74.3 jit_solution(10975009119810954326)
XLA Ops:
  0.6 0.0 copy-start
  0.6 1.0 %copy-done = f32[16,64,128]{2,1,0:T(8,128)S(1)} copy-done((f32[16,64,128]{2,1,0:T(8,128)S(1)}, f32[16,64,128]{2,1,0:T(8,128)}, u32[]{:S(2)}) %copy-start) | copy-done | bytes 524312
  1.7 0.0 copy-start.1
  1.7 1.0 %copy-done.1 = f32[16,64,128]{2,1,0:T(8,128)S(1)} copy-done((f32[16,64,128]{2,1,0:T(8,128)S(1)}, f32[16,64,128]{2,1,0:T(8,128)}, u32[]{:S(2)}) %copy-start.1) | copy-done | bytes 524312
  2.7 0.0 copy-start.2
  2.7 0.9 %copy-done.2 = f32[3,128,128]{2,1,0:T(8,128)S(1)} copy-done((f32[3,128,128]{2,1,0:T(8,128)S(1)}, f32[3,128,128]{2,1,0:T(8,128)}, u32[]{:S(2)}) %copy-start.2) | copy-done | bytes 196632
  3.6 0.0 copy-start.3
  3.6 0.9 %copy-done.3 = f32[3,128,128]{2,1,0:T(8,128)S(1)} copy-done((f32[3,128,128]{2,1,0:T(8,128)S(1)}, f32[3,128,128]{2,1,0:T(8,128)}, u32[]{:S(2)}) %copy-start.3) | copy-done | bytes 196632
  4.6 0.0 copy-start.4
  4.6 0.7 copy-done.4
  5.3 66.9 %shard_map.76 = (f32[16,64,128]{2,1,0:T(8,128)S(1)}, f32[128,128]{1,0:T(8,128)S(1)}, f32[4,48,128]{2,1,0:T(8,128)S(1)}) custom-call(f32[16,64,128]{2,1,0:T(8,128)S(1)} %copy-done, f32[16,64,128]{2,1,0:T(8,128)S(1)} %copy-done.1, f32[3,128,128]{2,1,0:T(8,128)S(1)} %copy-done.2, f32[384,128]{1,0:T(8,128)S(1)} %bitcast.2, f32[3,3,3,16]{3,2,1,0:T(4,128)S(1)} %copy-done.4), custom_call_target="tpu_custom_call" | custom-call | tf_op jit(solution)/shard_map/pallas_call | solution.py:500
  72.2 0.8 %copy.11 = f32[16,64,128]{2,1,0:T(8,128)} copy(f32[16,64,128]{2,1,0:T(8,128)S(1)} %get-tuple-element.12) | data formatting | bytes 1048576
  73.0 0.6 copy.12
  73.6 0.6 copy.13
Async XLA Ops:
  0.6 1.0 %copy-start = (f32[16,64,128]{2,1,0:T(8,128)S(1)}, f32[16,64,128]{2,1,0:T(8,128)}, u32[]{:S(2)}) copy-start(f32[16,64,128]{2,1,0:T(8,128)} %x_ref.1) | copy-start | bytes 1572868
  1.7 1.0 %copy-start.1 = (f32[16,64,128]{2,1,0:T(8,128)S(1)}, f32[16,64,128]{2,1,0:T(8,128)}, u32[]{:S(2)}) copy-start(f32[16,64,128]{2,1,0:T(8,128)} %f_ref.1) | copy-start | bytes 1572868
  2.7 0.9 %copy-start.2 = (f32[3,128,128]{2,1,0:T(8,128)S(1)}, f32[3,128,128]{2,1,0:T(8,128)}, u32[]{:S(2)}) copy-start(f32[3,128,128]{2,1,0:T(8,128)} %l_hbm.1) | copy-start | bytes 589828
  3.6 0.9 %copy-start.3 = (f32[3,128,128]{2,1,0:T(8,128)S(1)}, f32[3,128,128]{2,1,0:T(8,128)}, u32[]{:S(2)}) copy-start(f32[3,128,128]{2,1,0:T(8,128)} %param.8) | copy-start | bytes 589828
  4.6 0.7 copy-start.4

commit v2 on v1

--- a/solution.py
+++ b/solution.py
@@ -8,7 +8,6 @@
 from jax.sharding import PartitionSpec as P
 
 HIGH = lax.Precision.HIGH
-HIGHEST = lax.Precision.HIGHEST
 F32 = jnp.float32
 
 
@@ -56,7 +55,7 @@
         base = k * size
         panel = work[base : base + size, :]
         rows = [jnp.broadcast_to(panel[i : i + 1, :], (size, 2 * width)) for i in range(size)]
-        entry = {}
+        entry, factors, inverses = {}, {}, []
         for j in range(size):
             column = jnp.broadcast_to(panel[:, base + j : base + j + 1], (size, width))
             for i in range(j, size):
@@ -66,7 +65,10 @@
             inv = lax.rsqrt(pivot)
             inv = inv * (1.5 - 0.5 * (pivot * inv) * inv)
             rows[j] = rows[j] * jnp.concatenate([inv, inv], axis=1)
+            inverses.append(inv)
             scaled = {i: entry[i, j] * inv for i in range(j + 1, size)}
+            for i in scaled:
+                factors[i, j] = scaled[i]
             for c in range(j + 1, size):
                 for i in range(c, size):
                     entry[i, c] = entry[i, c] - scaled[i] * scaled[c]
@@ -77,9 +79,17 @@
         for i in range(1, size):
             done = jnp.where(sub == i, rows[i], done)
         work[base : base + size, :] = done
-        if base + size < width:
-            update = dot(done[:, :width], done, ((0,), (0,)), HIGHEST)
-            work[base + size :, :] = work[base + size :, :] - update[base + size :, :]
+        for start in range(base + size, width, size):
+            block = work[start : start + size, :]
+            lower = []
+            for j in range(size):
+                column = jnp.broadcast_to(block[:, base + j : base + j + 1], (size, width))
+                for c in range(j):
+                    column = column - lower[c] * factors[j, c]
+                lower.append(column * inverses[j])
+            for j in range(size):
+                block = block - jnp.concatenate([lower[j], lower[j]], axis=1) * rows[j]
+            work[start : start + size, :] = block
 
 
 def kernel(
@@ -269,20 +279,21 @@
 
     fetch_p.wait()
     contract_right(xf, p_ref, tt, mine + 4, width)
-    arrive(ff, 1, f_recv, fe_recv, f_send, fe_send, own_sem.at[3])
 
     def applied(index, row):
         pair = coupled_pair(tt, ce, row, index, False, width)
         stacked = jnp.concatenate([jnp.concatenate(parts, axis=1) for parts in pair], axis=0)
         return dot(stacked, lt_rows[...])
 
-    def residual_body(p, carry):
+    def applied_body(p, carry):
         out = applied(2 * p, 2 * p)
-        res[2 * p] = ff[2 * p] - out[:width]
-        res[2 * p + 1] = ff[2 * p + 1] - out[width:]
+        res[2 * p] = out[:width]
+        res[2 * p + 1] = out[width:]
         return carry
 
-    lax.fori_loop(0, (mine + 2) // 2, residual_body, 0)
+    lax.fori_loop(0, (mine + 2) // 2, applied_body, 0)
+    arrive(ff, 1, f_recv, fe_recv, f_send, fe_send, own_sem.at[3])
+    res[...] = ff[...] - res[...]
 
     def gram_body(p, total):
         i = 2 * p
@@ -504,11 +515,11 @@
             jax.ShapeDtypeStruct((width, width), F32),
             jax.ShapeDtypeStruct((ml, nrows, width), F32),
         ),
-        in_specs=[pl.BlockSpec(memory_space=pl.ANY)] * 4 + [space],
+        in_specs=[pl.BlockSpec(memory_space=pltpu.HBM)] * 4 + [space],
         out_specs=(space,) * 3,
         scratch_shapes=scratch,
         compiler_params=pltpu.CompilerParams(
-            collective_id=0, has_side_effects=True, vmem_limit_bytes=40 * 1024 * 1024
+            collective_id=0, has_side_effects=True, vmem_limit_bytes=60 * 1024 * 1024
         ),
     )(
         start_core, right_side, left_interface,

time: 74.6 us -> 66.3 us (0.89)
  Pallas kernels: 66.9 us -> 61.9 us
  local copies, waits for them, and re-layouts: 6.71 us -> 3.48 us
    pallas_call x1, Pallas kernels: 66.9 us -> 61.9 us  [shards(): pl.pallas_call(functools.partial(kernel, nm, nr, ml, scale), out_shape=(j...]
    unnamed x13 -> x7, local copies, waits for them, and re-layouts: 6.71 us -> 3.48 us
where the time goes in v2:
time: 66.3 us; the launch traced here: 66.1 us
  Pallas kernels  61.9 us (93%)
  local copies, waits for them, and re-layouts  3.48 us (5%)
    pallas_call x1, Pallas kernels, shards(): pl.pallas_call(functools.partial(kernel, nm, nr, ml, scale), out_shape=(j...  61.9 us
    unnamed x7, local copies, waits for them, and re-layouts  3.48 us

profile of v2, /device:TPU:0, one launch (start us, length us, event | category | flops | bytes accessed | tf_op | source)
XLA Modules:
  0.0 66.1 jit_solution(8837634306203661589)
XLA Ops:
  0.6 61.9 %shard_map.76 = (f32[16,64,128]{2,1,0:T(8,128)}, f32[128,128]{1,0:T(8,128)}, f32[4,48,128]{2,1,0:T(8,128)}) custom-call(f32[16,64,128]{2,1,0:T(8,128)} %x_ref.1, f32[16,64,128]{2,1,0:T(8,128)} %f_ref.1, f32[3,128,128]{2,1,0:T(8,128)} %l_hbm.1, f32[384,128]{1,0:T(8,128)} %bitcast.2, f32[3,3,3,16]{3,2,1,0:T(4,128)} %raw_ref.1), custom_call_target="tpu_custom_call" | custom-call | tf_op jit(solution)/shard_map/pallas_call | solution.py:511
  62.6 0.0 copy-start.1
  62.6 1.9 %copy.11 = f32[16,64,128]{2,1,0:T(8,128)} copy(f32[16,64,128]{2,1,0:T(8,128)} %get-tuple-element.12) | data formatting | bytes 1048576
  64.5 0.0 copy-done.1
  64.5 0.0 copy-start
  64.5 0.6 copy.12
  65.1 0.3 copy-done
  65.4 0.6 copy.13
Async XLA Ops:
  62.6 1.9 %copy-start.1 = (f32[128,128]{1,0:T(8,128)S(1)}, f32[128,128]{1,0:T(8,128)}, u32[]{:S(2)}) copy-start(f32[128,128]{1,0:T(8,128)} %get-tuple-element.13) | copy-start | bytes 196612
  64.5 0.9 %copy-start = (f32[4,48,128]{2,1,0:T(8,128)S(1)}, f32[4,48,128]{2,1,0:T(8,128)}, u32[]{:S(2)}) copy-start(f32[4,48,128]{2,1,0:T(8,128)} %get-tuple-element.8) | copy-start | bytes 294916

commit v3 on v2

--- a/solution.py
+++ b/solution.py
@@ -8,6 +8,7 @@
 from jax.sharding import PartitionSpec as P
 
 HIGH = lax.Precision.HIGH
+HIGHEST = lax.Precision.HIGHEST
 F32 = jnp.float32
 
 
@@ -48,10 +49,10 @@
     return [coupled(field, factors, row + d, index + d, inner_first, width) for d in range(2)]
 
 
-def eliminate(work, width):
+def eliminate(work, width, begin, end):
     size = 8
     sub = lax.broadcasted_iota(jnp.int32, (size, 2 * width), 0)
-    for k in range(width // size):
+    for k in range(begin, end):
         base = k * size
         panel = work[base : base + size, :]
         rows = [jnp.broadcast_to(panel[i : i + 1, :], (size, 2 * width)) for i in range(size)]
@@ -97,7 +98,7 @@
     x_ref, f_ref, l_hbm, p_hbm, raw_ref,
     q_out, tri_out, n_out,
     l_ref, p_ref, c_ref, own_sem,
-    xf, ff, ce, tt, res, qb, lt_rows, lt_cols, work,
+    xf, ff, ce, tt, res, qb, cfull, lt_rows, lt_cols, work,
     gpart, grecv, gsend, gbrecv, gfull,
     ssend, srecv, sbsend, sbrecv,
     npart, nrecv, nsend, nbrecv, nfull,
@@ -392,26 +393,16 @@
     lanes = lax.broadcasted_iota(jnp.int32, (width, width), 1)
     work[:, :width] = gram
     work[:, width:] = jnp.where(rows == lanes, 1.0, 0.0).astype(F32)
-    eliminate(work, width)
-    tri_out[...] = jnp.where(lanes >= rows, work[:, :width], 0.0)
-    inverse = jnp.where(lanes <= rows, work[:, width:], 0.0)
-
-    def basis_body(p, carry):
-        pair = jnp.concatenate(
-            [xf[2 * p + 1] + alpha * res[2 * p], xf[2 * p + 2] + alpha * res[2 * p + 1]], axis=1
-        )
-        out = dot(inverse, pair)
-        qb[2 * p] = out[:, :width]
-        qb[2 * p + 1] = out[:, width:]
+    def core_body(i, carry):
+        qb[i] = xf[i + 1] + alpha * res[i]
         return carry
 
-    lax.fori_loop(0, (mine + 2) // 2, basis_body, 0)
+    lax.fori_loop(0, mine + 2, core_body, 0)
     slab = pl.ds(r * mine, mine)
     for d in range(1, nr):
         t = lax.rem(r + d, nr)
         remote(
-            qb.at[pl.ds(1, mine), pl.ds(pl.multiple_of(t * piece, piece), piece)],
-            q_out.at[slab], q_send.at[d - 1], q_recv.at[d - 1], at_r(t),
+            qb.at[pl.ds(1, mine)], cfull.at[slab], q_send.at[d - 1], q_recv.at[d - 1], at_r(t)
         ).start()
 
     def mixed_body(p, carry):
@@ -427,39 +418,49 @@
         i = 2 * p
         pair = coupled_pair(tt, ce, i + 1, i, True, width)
         moved = jnp.concatenate([jnp.concatenate(parts, axis=0) for parts in pair], axis=1)
-        basis = jnp.concatenate([qb[i + 1], qb[i + 2]], axis=1)
-        return total + dot(moved, basis, ((1,), (1,)))
+        fields = jnp.concatenate([qb[i + 1], qb[i + 2]], axis=1)
+        return total + dot(moved, fields, ((1,), (1,)))
 
     total = lax.fori_loop(0, mine // 2, interface_body, jnp.zeros((3 * width, width), F32)) * scale
-    total = total.reshape(3, nr, piece, width)
-    for t in range(nr):
-        npart[t * ml : (t + 1) * ml] = total[:, t].reshape((ml,) + npart.shape[1:])
+    npart[...] = total.reshape(npart.shape)
     scatter(npart, nrecv, na_send, na_recv)
-    q_out[slab] = qb[1 : mine + 1, columns, :]
+    cfull[slab] = qb[1 : mine + 1]
+
+    blocks = width // 8
+    stops = [0, blocks * 3 // 8, blocks * 5 // 8, blocks]
+    eliminate(work, width, stops[0], stops[1])
     gathered(nrecv, na_send, na_recv)
     nsend[...] = add_up(nrecv, na)
     exchange_b(nsend, nbrecv, nb_send, nb_recv)
+    eliminate(work, width, stops[1], stops[2])
     gathered_b(nbrecv, nb_send, nb_recv)
-    nfull[low] = add_up(nbrecv, mh)
-
-    def at_c(t):
-        return {"mode": high * ml + t, "rank": r}
-
-    for d in range(1, ml):
-        t = lax.rem(low + d, ml)
-        remote(
-            nfull.at[low], nfull.at[low], nc_send.at[d - 1], nc_recv.at[d - 1], at_c(t)
-        ).start()
-    for d in range(1, ml):
-        t = lax.rem(low + ml - d, ml)
-        block = nfull.at[t]
-        remote(block, block, nc_send.at[d - 1], nc_recv.at[d - 1], at_c(t)).wait_recv()
-    n_out[...] = nfull[...]
+    nfull[g] = add_up(nbrecv, mh)
+    for d in range(1, na):
+        t = lax.rem(g + d, na)
+        remote(nfull.at[g], nfull.at[g], nc_send.at[d - 1], nc_recv.at[d - 1], at_a(t)).start()
+    eliminate(work, width, stops[2], stops[3])
+    tri_out[...] = jnp.where(lanes >= rows, work[:, :width], 0.0)
+    inverse = jnp.where(lanes <= rows, work[:, width:], 0.0)
+    work[:, width:] = inverse
+    owned = work[columns, width:]
 
     for d in range(1, nr):
         t = lax.rem(r + nr - d, nr)
-        block = q_out.at[pl.ds(t * mine, mine)]
+        block = cfull.at[pl.ds(t * mine, mine)]
         remote(block, block, q_send.at[d - 1], q_recv.at[d - 1], at_r(t)).wait_recv()
+
+    def basis_body(p, carry):
+        out = dot(owned, jnp.concatenate([cfull[2 * p], cfull[2 * p + 1]], axis=1))
+        q_out[2 * p] = out[:, :width]
+        q_out[2 * p + 1] = out[:, width:]
+        return carry
+
+    lax.fori_loop(0, height // 2, basis_body, 0)
+    gathered(nfull, nc_send, nc_recv)
+    sums = nfull[...].reshape(3 * width, width)
+    for k in range(3):
+        half = dot(owned, sums[k * width : (k + 1) * width], precision=HIGHEST)
+        n_out[k] = dot(half, inverse, ((1,), (1,)), HIGHEST)
 
     for up, down, across in moves:
         pl.when(has_next)(up.wait_send)
@@ -471,7 +472,7 @@
     for send, block, count in (
         (ga_send, gpart.at[0], na), (gc_send, gfull.at[0], na), (sa_send, ssend, na),
         (na_send, npart.at[0], na), (gb_send, gsend, mh), (sb_send, sbsend, mh),
-        (nb_send, nsend, mh), (nc_send, nfull.at[0], ml), (q_send, q_out.at[pl.ds(0, mine)], nr),
+        (nb_send, nsend, mh), (nc_send, nfull.at[0], na), (q_send, cfull.at[pl.ds(0, mine)], nr),
     ):
         for d in range(1, count):
             remote(block, block, send.at[d - 1], send.at[d - 1], at_r(r)).wait_send()
@@ -485,26 +486,26 @@
     na = nr * ml
     scale = 1.0 / (height * nm * width)
     grows = 3 * width // na
-    nrows = 3 * piece // ml
     vmem = lambda *shape: pltpu.VMEM(shape, F32)
     sem = lambda count: pltpu.SemaphoreType.DMA((max(1, count),))
     scratch = [
         vmem(3, width, width), vmem(3 * width, width), vmem(height, 27, width), sem(4),
         vmem(mine + 4, width, width), vmem(mine + 2, width, width), vmem(mine + 2, 27, width),
         vmem(3, mine + 4, width, width), vmem(mine + 2, width, width),
-        vmem(mine + 2, width, width), vmem(3 * width, width), vmem(width, 3 * width),
+        vmem(mine + 2, width, width), vmem(height, width, width),
+        vmem(3 * width, width), vmem(width, 3 * width),
         vmem(width, 2 * width),
         vmem(na, grows, width), vmem(na, grows, width), vmem(grows, width),
         vmem(mh, grows, width), vmem(na, grows, width),
         vmem(8, width), vmem(na, 8, width), vmem(8, width), vmem(mh, 8, width),
-        vmem(na, nrows, width), vmem(na, nrows, width), vmem(nrows, width),
-        vmem(mh, nrows, width), vmem(ml, nrows, width),
+        vmem(na, grows, width), vmem(na, grows, width), vmem(grows, width),
+        vmem(mh, grows, width), vmem(na, grows, width),
         sem(nr), sem(nr), sem(2), sem(nr),
         sem(nr), sem(nr), sem(2), sem(nr),
         sem(2), sem(2),
         sem(na), sem(na), sem(mh), sem(mh), sem(na), sem(na),
         sem(na), sem(na), sem(mh), sem(mh),
-        sem(na), sem(na), sem(mh), sem(mh), sem(ml), sem(ml),
+        sem(na), sem(na), sem(mh), sem(mh), sem(na), sem(na),
         sem(nr), sem(nr),
     ]
     space = pl.BlockSpec(memory_space=pltpu.VMEM)
@@ -513,7 +514,7 @@
         out_shape=(
             jax.ShapeDtypeStruct((height, piece, width), F32),
             jax.ShapeDtypeStruct((width, width), F32),
-            jax.ShapeDtypeStruct((ml, nrows, width), F32),
+            jax.ShapeDtypeStruct((3, piece, width), F32),
         ),
         in_specs=[pl.BlockSpec(memory_space=pltpu.HBM)] * 4 + [space],
         out_specs=(space,) * 3,
@@ -525,7 +526,7 @@
         start_core, right_side, left_interface,
         right_interface.reshape(3 * width, width), couplings,
     )
-    return basis, triangle, interface.reshape(3, piece, width)
+    return basis, triangle, interface
 
 
 def solution(mesh):

time: 66.3 us -> 67.3 us (1.015)
  Pallas kernels: 61.9 us -> 62.9 us
    pallas_call x1, Pallas kernels: 61.9 us -> 62.9 us  [shards(): pl.pallas_call(functools.partial(kernel, nm, nr, ml, scale), out_shape=(j...]
where the time goes in v3:
time: 67.3 us; the launch traced here: 67 us
  Pallas kernels  62.9 us (93%)
  local copies, waits for them, and re-layouts  3.48 us (5%)
    pallas_call x1, Pallas kernels, shards(): pl.pallas_call(functools.partial(kernel, nm, nr, ml, scale), out_shape=(j...  62.9 us
    unnamed x7, local copies, waits for them, and re-layouts  3.48 us

profile of v3, /device:TPU:0, one launch (start us, length us, event | category | flops | bytes accessed | tf_op | source)
XLA Modules:
  0.0 67.0 jit_solution(1286212802205174152)
XLA Ops:
  0.6 62.9 %shard_map.76 = (f32[16,64,128]{2,1,0:T(8,128)}, f32[128,128]{1,0:T(8,128)}, f32[3,64,128]{2,1,0:T(8,128)}) custom-call(f32[16,64,128]{2,1,0:T(8,128)} %x_ref.1, f32[16,64,128]{2,1,0:T(8,128)} %f_ref.1, f32[3,128,128]{2,1,0:T(8,128)} %l_hbm.1, f32[384,128]{1,0:T(8,128)} %bitcast.1, f32[3,3,3,16]{3,2,1,0:T(4,128)} %raw_ref.1), custom_call_target="tpu_custom_call" | custom-call | tf_op jit(solution)/shard_map/pallas_call | solution.py:512
  63.5 0.0 copy-start.1
  63.5 1.9 %copy.11 = f32[16,64,128]{2,1,0:T(8,128)} copy(f32[16,64,128]{2,1,0:T(8,128)} %get-tuple-element.6) | data formatting | bytes 1048576
  65.5 0.0 copy-done.1
  65.5 0.0 copy-start
  65.5 0.6 copy.12
  66.1 0.3 copy-done
  66.4 0.6 copy.13
Async XLA Ops:
  63.5 1.9 %copy-start.1 = (f32[128,128]{1,0:T(8,128)S(1)}, f32[128,128]{1,0:T(8,128)}, u32[]{:S(2)}) copy-start(f32[128,128]{1,0:T(8,128)} %get-tuple-element.7) | copy-start | bytes 196612
  65.5 0.9 %copy-start = (f32[3,64,128]{2,1,0:T(8,128)S(1)}, f32[3,64,128]{2,1,0:T(8,128)}, u32[]{:S(2)}) copy-start(f32[3,64,128]{2,1,0:T(8,128)} %get-tuple-element.8) | copy-start | bytes 294916

commit v4 on v3

--- a/solution.py
+++ b/solution.py
@@ -98,7 +98,7 @@
     x_ref, f_ref, l_hbm, p_hbm, raw_ref,
     q_out, tri_out, n_out,
     l_ref, p_ref, c_ref, own_sem,
-    xf, ff, ce, tt, res, qb, cfull, lt_rows, lt_cols, work,
+    xf, ff, ce, tt, res, qb, cfull, qlate, lt_rows, lt_cols, work,
     gpart, grecv, gsend, gbrecv, gfull,
     ssend, srecv, sbsend, sbrecv,
     npart, nrecv, nsend, nbrecv, nfull,
@@ -108,7 +108,7 @@
     ga_send, ga_recv, gb_send, gb_recv, gc_send, gc_recv,
     sa_send, sa_recv, sb_send, sb_recv,
     na_send, na_recv, nb_send, nb_recv, nc_send, nc_recv,
-    q_send, q_recv,
+    q_send, q_recv, e_send, e_recv,
 ):
     height, piece, width = x_ref.shape
     mine = height // nr
@@ -398,11 +398,12 @@
         return carry
 
     lax.fori_loop(0, mine + 2, core_body, 0)
-    slab = pl.ds(r * mine, mine)
+    early = cfull.shape[1]
+    late = mine - early
     for d in range(1, nr):
         t = lax.rem(r + d, nr)
         remote(
-            qb.at[pl.ds(1, mine)], cfull.at[slab], q_send.at[d - 1], q_recv.at[d - 1], at_r(t)
+            qb.at[pl.ds(1, early)], cfull.at[r], e_send.at[d - 1], e_recv.at[d - 1], at_r(t)
         ).start()
 
     def mixed_body(p, carry):
@@ -424,7 +425,7 @@
     total = lax.fori_loop(0, mine // 2, interface_body, jnp.zeros((3 * width, width), F32)) * scale
     npart[...] = total.reshape(npart.shape)
     scatter(npart, nrecv, na_send, na_recv)
-    cfull[slab] = qb[1 : mine + 1]
+    cfull[r] = qb[1 : early + 1]
 
     blocks = width // 8
     stops = [0, blocks * 3 // 8, blocks * 5 // 8, blocks]
@@ -444,23 +445,35 @@
     work[:, width:] = inverse
     owned = work[columns, width:]
 
+    for j in range(late):
+        qlate[j] = dot(inverse, qb[early + 1 + j])
+    own_late = pl.ds(r * mine + early, late)
+    for d in range(1, nr):
+        t = lax.rem(r + d, nr)
+        remote(
+            qlate.at[:, pl.ds(pl.multiple_of(t * piece, piece), piece)],
+            q_out.at[own_late], q_send.at[d - 1], q_recv.at[d - 1], at_r(t),
+        ).start()
+    q_out[own_late] = qlate[:, columns, :]
+
     for d in range(1, nr):
         t = lax.rem(r + nr - d, nr)
-        block = cfull.at[pl.ds(t * mine, mine)]
-        remote(block, block, q_send.at[d - 1], q_recv.at[d - 1], at_r(t)).wait_recv()
-
-    def basis_body(p, carry):
-        out = dot(owned, jnp.concatenate([cfull[2 * p], cfull[2 * p + 1]], axis=1))
-        q_out[2 * p] = out[:, :width]
-        q_out[2 * p + 1] = out[:, width:]
-        return carry
-
-    lax.fori_loop(0, height // 2, basis_body, 0)
+        block = cfull.at[t]
+        remote(block, block, e_send.at[d - 1], e_recv.at[d - 1], at_r(t)).wait_recv()
+    for j in range(early):
+        out = dot(owned, jnp.concatenate([cfull[t, j] for t in range(nr)], axis=1))
+        for t in range(nr):
+            q_out[t * mine + j] = out[:, t * width : (t + 1) * width]
     gathered(nfull, nc_send, nc_recv)
     sums = nfull[...].reshape(3 * width, width)
     for k in range(3):
         half = dot(owned, sums[k * width : (k + 1) * width], precision=HIGHEST)
         n_out[k] = dot(half, inverse, ((1,), (1,)), HIGHEST)
+
+    for d in range(1, nr):
+        t = lax.rem(r + nr - d, nr)
+        block = q_out.at[pl.ds(t * mine + early, late)]
+        remote(block, block, q_send.at[d - 1], q_recv.at[d - 1], at_r(t)).wait_recv()
 
     for up, down, across in moves:
         pl.when(has_next)(up.wait_send)
@@ -472,7 +485,8 @@
     for send, block, count in (
         (ga_send, gpart.at[0], na), (gc_send, gfull.at[0], na), (sa_send, ssend, na),
         (na_send, npart.at[0], na), (gb_send, gsend, mh), (sb_send, sbsend, mh),
-        (nb_send, nsend, mh), (nc_send, nfull.at[0], na), (q_send, cfull.at[pl.ds(0, mine)], nr),
+        (nb_send, nsend, mh), (nc_send, nfull.at[0], na), (q_send, q_out.at[pl.ds(0, late)], nr),
+        (e_send, cfull.at[0], nr),
     ):
         for d in range(1, count):
             remote(block, block, send.at[d - 1], send.at[d - 1], at_r(r)).wait_send()
@@ -492,7 +506,8 @@
         vmem(3, width, width), vmem(3 * width, width), vmem(height, 27, width), sem(4),
         vmem(mine + 4, width, width), vmem(mine + 2, width, width), vmem(mine + 2, 27, width),
         vmem(3, mine + 4, width, width), vmem(mine + 2, width, width),
-        vmem(mine + 2, width, width), vmem(height, width, width),
+        vmem(mine + 2, width, width),
+        vmem(nr, mine // 2, width, width), vmem(mine - mine // 2, width, width),
         vmem(3 * width, width), vmem(width, 3 * width),
         vmem(width, 2 * width),
         vmem(na, grows, width), vmem(na, grows, width), vmem(grows, width),
@@ -506,7 +521,7 @@
         sem(na), sem(na), sem(mh), sem(mh), sem(na), sem(na),
         sem(na), sem(na), sem(mh), sem(mh),
         sem(na), sem(na), sem(mh), sem(mh), sem(na), sem(na),
-        sem(nr), sem(nr),
+        sem(nr), sem(nr), sem(nr), sem(nr),
     ]
     space = pl.BlockSpec(memory_space=pltpu.VMEM)
     basis, triangle, interface = pl.pallas_call(

time: 67.3 us -> 63.2 us (0.939)
  Pallas kernels: 62.9 us -> 58.8 us
    pallas_call x1, Pallas kernels: 62.9 us -> 58.8 us  [shards(): pl.pallas_call(functools.partial(kernel, nm, nr, ml, scale), out_shape=(j...]
where the time goes in v4:
time: 63.2 us; the launch traced here: 62.9 us
  Pallas kernels  58.8 us (93%)
  local copies, waits for them, and re-layouts  3.48 us (6%)
  between operations  0.65 us (1%)
    pallas_call x1, Pallas kernels, shards(): pl.pallas_call(functools.partial(kernel, nm, nr, ml, scale), out_shape=(j...  58.8 us
    unnamed x7, local copies, waits for them, and re-layouts  3.48 us

profile of v4, /device:TPU:0, one launch (start us, length us, event | category | flops | bytes accessed | tf_op | source)
XLA Modules:
  0.0 62.9 jit_solution(3047358168350838517)
XLA Ops:
  0.6 58.8 %shard_map.76 = (f32[16,64,128]{2,1,0:T(8,128)}, f32[128,128]{1,0:T(8,128)}, f32[3,64,128]{2,1,0:T(8,128)}) custom-call(f32[16,64,128]{2,1,0:T(8,128)} %x_ref.1, f32[16,64,128]{2,1,0:T(8,128)} %f_ref.1, f32[3,128,128]{2,1,0:T(8,128)} %l_hbm.1, f32[384,128]{1,0:T(8,128)} %bitcast.1, f32[3,3,3,16]{3,2,1,0:T(4,128)} %raw_ref.1), custom_call_target="tpu_custom_call" | custom-call | tf_op jit(solution)/shard_map/pallas_call | solution.py:527
  59.4 0.0 copy-start.1
  59.5 1.9 %copy.11 = f32[16,64,128]{2,1,0:T(8,128)} copy(f32[16,64,128]{2,1,0:T(8,128)} %get-tuple-element.6) | data formatting | bytes 1048576
  61.4 0.0 copy-done.1
  61.4 0.0 copy-start
  61.4 0.6 %copy.12 = f32[128,128]{1,0:T(8,128)} copy(f32[128,128]{1,0:T(8,128)S(1)} %copy-done.1) | data formatting | bytes 131072
  62.0 0.3 copy-done
  62.3 0.6 %copy.13 = f32[3,64,128]{2,1,0:T(8,128)} copy(f32[3,64,128]{2,1,0:T(8,128)S(1)} %copy-done) | data formatting | bytes 196608
Async XLA Ops:
  59.4 1.9 %copy-start.1 = (f32[128,128]{1,0:T(8,128)S(1)}, f32[128,128]{1,0:T(8,128)}, u32[]{:S(2)}) copy-start(f32[128,128]{1,0:T(8,128)} %get-tuple-element.7) | copy-start | bytes 196612
  61.4 0.9 %copy-start = (f32[3,64,128]{2,1,0:T(8,128)S(1)}, f32[3,64,128]{2,1,0:T(8,128)}, u32[]{:S(2)}) copy-start(f32[3,64,128]{2,1,0:T(8,128)} %get-tuple-element.8) | copy-start | bytes 294916
